TPU v7x, 32 devices: a whole 2x2x4 slice. The times are simulated.
32 devices in a mesh: grp: 4 (over z), dom: 2 (over y), rel: 4 (over x, core).
Axes of the slice: x: 2, y: 2, z: 4, core: 2. Of those that a mesh axis runs over, the one named last changes fastest.
Arguments:
- features: bfloat16 [8192, 768], P(('grp', 'dom', 'rel')), may hold values from -6 to 6
- send_list: int32 [32, 2, 1], P(('grp', 'dom', 'rel')), may hold values from 0 to 1
- tile_values: bfloat16 [32, 2, 4, 128, 128], P(('grp', 'dom', 'rel')), may hold values from -0.1875 to 0.1875
- tile_meta: int32 [32, 2, 4, 4], P(('grp', 'dom', 'rel')), may hold values from 0 to 4, as said below
- rel_weight: bfloat16 [5, 768, 1024], replicated, may hold values from -0.21875 to 0.21875
- self_weight: bfloat16 [768, 1024], replicated, may hold values from -0.21875 to 0.21875
- bn_gain: float32 [1024], replicated, may hold values from 0.25 to 1.75
- bn_shift: float32 [1024], replicated, may hold values from -3 to 3
Outputs:
- activated: bfloat16 [8192, 1024], P(('grp', 'dom', 'rel'))
Inputs may be any that keep to these rules, and one draw needn't show every extreme that they name: `tile_meta`: entry [p, d, r] describes the tile that partition p holds for the partition of its group with dom index d and rel index r: relation below 5, destination block below 2, source table entry below 4, live flag 0 or 1. The live tiles received by one partition have distinct (relation, destination, source); in every group some partition receives only live tiles.
All inputs are finite; a program needn't handle non-finite values.
Results may differ from a plain program's by a relative error of at most 0.003.
Values may be sent and summed in bfloat16 or wider, within the bound.
A program may use at most 128 MiB of HBM per device.

v0:
```python
import jax
import jax.numpy as jnp
from jax import lax
from jax.sharding import PartitionSpec as P


def body(features, send_list, tile_values, tile_meta, rel_weight, self_weight, bn_gain, bn_shift):
    width = features.shape[1]
    block = tile_values.shape[-1]
    nblocks = features.shape[0] // block
    doms = lax.axis_size("dom")
    rels = lax.axis_size("rel")
    slots = doms * rels
    kinds = rel_weight.shape[0]
    blocks = features.reshape(nblocks, block, width)
    outgoing = blocks[send_list[0]]
    incoming = lax.all_to_all(outgoing, "dom", split_axis=0, concat_axis=0, tiled=True)
    table = jnp.concatenate([blocks, incoming.reshape(-1, block, width)], axis=0)
    self_term = jnp.dot(features, self_weight, preferred_element_type=jnp.float32)
    values, meta = (
        lax.all_to_all(
            tile_values.reshape(slots, block, block),
            ("dom", "rel"),
            split_axis=0,
            concat_axis=0,
            tiled=True,
        ),
        lax.all_to_all(
            tile_meta.reshape(slots, 4), ("dom", "rel"), split_axis=0, concat_axis=0, tiled=True
        ),
    )
    group_size = 16 if slots % 16 == 0 else slots
    steps_count = slots // group_size
    codes_all = jnp.arange(kinds * nblocks, dtype=jnp.int32)

    def accumulate(total, pieces):
        tile_group, meta_group = pieces
        sources = table[meta_group[:, 2]]
        message = jnp.einsum(
            "kij,kjf->kif", tile_group, sources, preferred_element_type=jnp.float32
        )
        code = meta_group[:, 0] * nblocks + meta_group[:, 1]
        select = (code[:, None] == codes_all[None, :]).astype(jnp.float32) * meta_group[
            :, 3:4
        ].astype(jnp.float32)
        total = total + jnp.einsum("kc,kif->cif", select, message, precision=lax.Precision.HIGHEST)
        return (total, None)

    start = jnp.zeros((kinds * nblocks, block, width), jnp.float32)
    summed, unused = lax.scan(
        accumulate,
        start,
        (
            values.reshape(steps_count, group_size, block, block),
            meta.reshape(steps_count, group_size, 4),
        ),
    )
    aggregated = summed.astype(jnp.bfloat16).reshape(kinds, nblocks * block, width)
    pre = self_term
    for kind in range(kinds):
        pre = pre + jnp.dot(aggregated[kind], rel_weight[kind], preferred_element_type=jnp.float32)
    total_rows = pre.shape[0] * lax.axis_size("grp") * doms * rels
    mean = lax.psum(jnp.sum(pre, axis=0), ("grp", "dom", "rel")) / total_rows
    centered = pre - mean
    variance = lax.psum(jnp.sum(centered * centered, axis=0), ("grp", "dom", "rel")) / total_rows
    normed = centered / jnp.sqrt(variance + 1e-05) * bn_gain + bn_shift
    return jax.nn.elu(normed).astype(jnp.bfloat16)


def solution(mesh):
    return jax.shard_map(
        body,
        mesh=mesh,
        in_specs=(
            P(("grp", "dom", "rel"), None),
            P(("grp", "dom", "rel"), None, None),
            P(("grp", "dom", "rel"), None, None, None, None),
            P(("grp", "dom", "rel"), None, None, None),
            P(),
            P(),
            P(),
            P(),
        ),
        out_specs=P(("grp", "dom", "rel"), None),
        check_vma=False,
    )
```

profile of v0, /device:TPU:0, one launch (start us, length us, event | category | flops | bytes accessed | tf_op | source)
XLA Modules:
  0.0 133.0 jit_solution(16779788910335750364)
XLA Ops:
  0.0 0.0 copy-start
  0.0 0.0 copy-start.2
  0.0 5.3 %all-to-all-start = ((s32[8,1,4]{2,1,0:T(1,128)}), s32[8,1,4]{2,1,0:T(1,128)S(1)}, u32[]{:S(2)}, u32[]{:S(2)}) async-start(s32[8,1,4]{2,1,0:T(1,128)} %bitcast.76), calls=%async_computation | async-start | bytes 8192 | tf_op jit(solution)/shard_map/all_to_all | solution.py:28
  5.3 0.7 fusion.37
  6.0 0.0 copy-done
  6.0 2.6 %fusion.42 = f32[256,1024]{1,0:T(8,128)} fusion(bf16[256,768]{1,0:T(8,128)(2,1)} %param.8, bf16[768,1024]{1,0:T(8,128)(2,1)S(1)} %copy-done), kind=kOutput, calls=%fused_computation.49 | convolution fusion | flops 402653184 | bytes 3014656 | tf_op jit(solution)/shard_map/dot_general | solution.py:19
  8.6 0.0 copy-done.2
  8.6 1.3 gather_fusion
  9.9 0.0 all-to-all-done
  9.9 3.5 %all-to-all-start.1 = ((bf16[2,1,128,768]{3,2,1,0:T(8,128)(2,1)}), bf16[2,1,128,768]{3,2,1,0:T(8,128)(2,1)S(1)}, u32[]{:S(2)}, u32[]{:S(2)}) async-start(bf16[2,1,128,768]{3,2,1,0:T(8,128)(2,1)} %bitcast.8), calls=%async_computation.1 | async-start | bytes 786432 | tf_op jit(solution)/shard_map/all_to_all | solution.py:17
  13.4 0.1 copy.18
  13.5 7.4 %all-to-all-done.1 = bf16[2,1,128,768]{3,2,1,0:T(8,128)(2,1)S(1)} async-done(((bf16[2,1,128,768]{3,2,1,0:T(8,128)(2,1)}), bf16[2,1,128,768]{3,2,1,0:T(8,128)(2,1)S(1)}, u32[]{:S(2)}, u32[]{:S(2)}) %all-to-all-start.1) | async-done | bytes 393248 | tf_op jit(solution)/shard_map/all_to_all | solution.py:17
  20.9 3.4 %all-to-all-start.2 = ((bf16[8,128,128]{2,1,0:T(8,128)(2,1)}), bf16[8,128,128]{2,1,0:T(8,128)(2,1)S(1)}, u32[]{:S(2)}, u32[]{:S(2)}) async-start(bf16[8,128,128]{2,1,0:T(8,128)(2,1)} %bitcast.11), calls=%async_computation.2 | async-start | bytes 524288 | tf_op jit(solution)/shard_map/all_to_all | solution.py:21
  24.3 0.1 pad_maximum_fusion
  24.4 1.8 %gather_fusion.1 = bf16[8,128,768]{2,1,0:T(8,128)(2,1)} fusion(bf16[4,128,768]{2,1,0:T(8,128)(2,1)S(1)} %pad_maximum_fusion, s32[1024]{0:T(1024)S(1)} %pad_clamp_fusion), kind=kCustom, calls=%fused_computation.1 | custom fusion | bytes 3145760 | tf_op jit(solution)/shard_map/while/body/eval_jaxpr/gather | solution.py:38
  26.2 5.0 %all-to-all-done.2 = bf16[8,128,128]{2,1,0:T(8,128)(2,1)S(1)} async-done(((bf16[8,128,128]{2,1,0:T(8,128)(2,1)}), bf16[8,128,128]{2,1,0:T(8,128)(2,1)S(1)}, u32[]{:S(2)}, u32[]{:S(2)}) %all-to-all-start.2) | async-done | bytes 262176 | tf_op jit(solution)/shard_map/all_to_all | solution.py:21
  31.1 3.7 %convolution_bitcast_fusion = f32[8,128,768]{1,2,0:T(8,128)} fusion(bf16[8,128,768]{2,1,0:T(8,128)(2,1)} %gather_fusion.1, bf16[8,128,128]{2,1,0:T(8,128)(2,1)S(1)} %all-to-all-done.2), kind=kOutput, calls=%fused_computation.5 | convolution fusion | flops 201326592 | bytes 4980736 | tf_op jit(solution)/shard_map/while/body/eval_jaxpr/kij,kjf->kif/dot_general | solution.py:39
  34.8 3.7 %copy.20 = f32[8,128,768]{2,0,1:T(8,128)} copy(f32[8,128,768]{1,2,0:T(8,128)} %convolution_bitcast_fusion) | data formatting | bytes 6291456 | tf_op jit(solution)/shard_map/while/body/eval_jaxpr/kij,kjf->kif/dot_general | solution.py:39
  38.5 0.0 slice-start
  38.5 7.0 %convolution_convert_fusion = bf16[10,128,768]{2,0,1:T(8,128)(2,1)S(1)} fusion(f32[8,128,768]{2,0,1:T(8,128)} %copy.20, f32[8]{0:T(128)S(1)} %get-tuple-element.29, s32[8]{0:T(128)S(1)} %get-tuple-element.28), kind=kOutput, calls=%fused_computation.4 | convolution fusion | flops 95355040 | bytes 5111872 | tf_op jit(solution)/shard_map/while/body/eval_jaxpr/kc,kif->cif/dot_general | solution.py:46
  45.6 0.0 slice-start.1
  45.6 1.4 %fusion.40 = (bf16[2,128,768]{2,0,1:T(2,128)(2,1)S(1)}, bf16[2,128,768]{2,0,1:T(2,128)(2,1)S(1)}, bf16[2,128,768]{2,0,1:T(2,128)(2,1)S(1)}, bf16[2,128,768]{2,0,1:T(2,128)(2,1)S(1)}, bf16[2,128,768]{2,0,1:T(2,128)(2,1)S(1)}) fusion(bf16[10,128,768]{2,0,1:T(8,128)(2,1)S(1)} %convolution_convert_fusion), kind=kLoop, calls=%fused_computation.47 | loop fusion | bytes 3932160 | tf_op jit(solution)/shard_map/slice | solution.py:61
  47.1 2.0 %fusion = f32[256,1024]{1,0:T(8,128)S(1)} fusion(bf16[256,768]{1,0:T(8,128)(2,1)S(1)} %bitcast.71, bf16[5,768,1024]{2,1,0:T(8,128)(2,1)} %param.12), kind=kOutput, calls=%fused_computation.6 | convolution fusion | flops 402653184 | bytes 3014656 | tf_op jit(solution)/shard_map/dot_general | solution.py:61
  49.1 0.0 slice-done
  49.1 0.0 slice-done.1
  49.1 0.6 fusion.2
  49.7 0.0 copy-start.1
  49.7 0.6 fusion.4
  50.4 0.6 fusion.6
  51.0 0.0 copy-done.1
  51.0 0.0 copy-start.3
  51.0 0.0 copy-start.4
  51.0 0.7 fusion.41
  51.8 39.5 %psum.14 = f32[1024]{0:T(1024)S(1)} all-reduce(f32[1024]{0:T(1024)S(1)} %get-tuple-element.31), channel_id=1, replica_groups=mesh['grp'=4,'dom'=2,'rel'=4] {'grp','dom','rel'}, use_global_device_ids=true, to_apply=%region_1.2 | all-reduce | flops 1024 | bytes 8192 | tf_op jit(solution)/shard_map/psum | solution.py:63
  91.3 0.1 multiply_reduce_fusion
  91.4 40.2 %psum.15 = f32[1024]{0:T(1024)S(1)} all-reduce(f32[1024]{0:T(1024)S(1)} %multiply_reduce_fusion), channel_id=1, replica_groups=mesh['grp'=4,'dom'=2,'rel'=4] {'grp','dom','rel'}, use_global_device_ids=true, to_apply=%region_3.4 | all-reduce | flops 1024 | bytes 8192 | tf_op jit(solution)/shard_map/psum | solution.py:65
  131.6 0.0 copy-done.3
  131.6 0.0 copy-done.4
  131.6 1.3 %fusion.31 = bf16[256,1024]{1,0:T(8,128)(2,1)} fusion(f32[256,1024]{1,0:T(8,128)S(1)} %get-tuple-element.32, f32[1024]{0:T(1024)S(1)} %copy-done.3, f32[1024]{0:T(1024)S(1)} %copy-done.4, f32[1024]{0:T(1024)S(1)} %add_sqrt_fusion, f32[1024]{0:T(1024)S(1)} %broadcast_multiply_fusion), kind=kLoop, calls=%fused_computation.27 | loop fusion | flops 2097152 | bytes 1589248 | tf_op jit(solution)/shard_map/convert_element_type | solution.py:67
  (11 shorter events, 0.2 us)
Async XLA Ops:
  0.0 6.0 %copy-start = (bf16[768,1024]{1,0:T(8,128)(2,1)S(1)}, bf16[768,1024]{1,0:T(8,128)(2,1)}, u32[]{:S(2)}) copy-start(bf16[768,1024]{1,0:T(8,128)(2,1)} %param.13) | copy-start | bytes 4718596
  0.0 8.6 %copy-start.2 = (bf16[256,768]{1,0:T(8,128)(2,1)S(1)}, bf16[256,768]{1,0:T(8,128)(2,1)}, u32[]{:S(2)}) copy-start(bf16[256,768]{1,0:T(8,128)(2,1)} %param.8) | copy-start | bytes 1179652
  0.0 9.9 %all-to-all-start = ((s32[8,1,4]{2,1,0:T(1,128)}), s32[8,1,4]{2,1,0:T(1,128)S(1)}, u32[]{:S(2)}, u32[]{:S(2)}) async-start(s32[8,1,4]{2,1,0:T(1,128)} %bitcast.76), calls=%async_computation | async-start | bytes 8192 | tf_op jit(solution)/shard_map/all_to_all | solution.py:28
  9.9 11.0 %all-to-all-start.1 = ((bf16[2,1,128,768]{3,2,1,0:T(8,128)(2,1)}), bf16[2,1,128,768]{3,2,1,0:T(8,128)(2,1)S(1)}, u32[]{:S(2)}, u32[]{:S(2)}) async-start(bf16[2,1,128,768]{3,2,1,0:T(8,128)(2,1)} %bitcast.8), calls=%async_computation.1 | async-start | bytes 786432 | tf_op jit(solution)/shard_map/all_to_all | solution.py:17
  20.9 10.3 %all-to-all-start.2 = ((bf16[8,128,128]{2,1,0:T(8,128)(2,1)}), bf16[8,128,128]{2,1,0:T(8,128)(2,1)S(1)}, u32[]{:S(2)}, u32[]{:S(2)}) async-start(bf16[8,128,128]{2,1,0:T(8,128)(2,1)} %bitcast.11), calls=%async_computation.2 | async-start | bytes 524288 | tf_op jit(solution)/shard_map/all_to_all | solution.py:21
  38.5 10.5 %slice-start = ((s8[7864320]{0:T(1024)(128)(4,1)}), s8[4194304]{0:T(1024)(128)(4,1)S(1)}, s32[]{:S(2)}) async-start(s8[7864320]{0:T(1024)(128)(4,1)} %bitcast.65), calls=%async_computation.3 | async-start | bytes 8388608
  45.6 3.5 %slice-start.1 = ((s8[7864320]{0:T(1024)(128)(4,1)}), s8[3670016]{0:T(1024)(128)(4,1)S(1)}, s32[]{:S(2)}) async-start(s8[7864320]{0:T(1024)(128)(4,1)} %bitcast.65), calls=%async_computation.4 | async-start | bytes 7340032
  49.7 1.3 copy-start.1
  51.0 80.6 %copy-start.3 = (f32[1024]{0:T(1024)S(1)}, f32[1024]{0:T(1024)}, u32[]{:S(2)}) copy-start(f32[1024]{0:T(1024)} %param.15) | copy-start | bytes 12292
  51.0 80.6 %copy-start.4 = (f32[1024]{0:T(1024)S(1)}, f32[1024]{0:T(1024)}, u32[]{:S(2)}) copy-start(f32[1024]{0:T(1024)} %param.14) | copy-start | bytes 12292
where the time goes:
time: 134 us; the launch traced here: 133 us
  blocking collectives  79.7 us (59%)
  matrix products  17.7 us (13%)
  waiting for transfers between devices  12.4 us (9%)
  starting transfers between devices  12.2 us (9%)
  local copies, waits for them, and re-layouts  8.5 us (6%)
  other arithmetic  2.23 us (2%)
    psum x1, blocking collectives, body(): lax.psum(jnp.sum(centered * centered, axis=0), ('grp', 'dom', 'rel'))  40.2 us
    psum x1, blocking collectives, body(): mean = lax.psum(jnp.sum(pre, axis=0), ('grp', 'dom', 'rel')) / total_rows  39.5 us
    all_to_all x1, waiting for transfers between devices, body(): lax.all_to_all(outgoing, 'dom', split_axis=0, concat_axis=0, tiled=True)  7.39 us
    dot_general x1, matrix products, accumulate(): jnp.einsum('kc,kif->cif', select, message, precision=lax.Precision.HIGHEST)  7.04 us
    all_to_all x1, starting transfers between devices, body(): lax.all_to_all(tile_meta.reshape(slots, 4), ('dom', 'rel'), split_axis=0,...  5.3 us
    all_to_all x1, waiting for transfers between devices, body(): lax.all_to_all(tile_values.reshape(slots, block, block), ('dom', 'rel'),...  4.97 us
    dot_general x5, matrix products, body(): jnp.dot(aggregated[kind], rel_weight[kind], preferred_element_type=jnp.fl...  4.43 us
    dot_general x1, matrix products, accumulate(): jnp.einsum('kij,kjf->kif', tile_group, sources, preferred_element_type=jn...  3.7 us
  transfers between devices with their start and end apart: 3, of which 2 were waited for; matrix products, arithmetic and copies ran while one was open for 5% of the time, Pallas kernels for 0%

commit v1 on v0

v1 whole, which is shorter than its diff:
```python
import functools

import jax
import jax.numpy as jnp
from jax import lax
from jax.experimental import pallas as pl
from jax.experimental.pallas import tpu as pltpu
from jax.sharding import PartitionSpec as P

MESH = pl.DeviceIdType.MESH
CODE_ROWS = 16
F_CHUNK = 256
COL_PARTS = 2


def repeat(count, body, static):
    if static:
        for index in range(count):
            body(index)
    else:

        @pl.loop(0, count)
        def _(index):
            body(index)


def aligned(index, size):
    return pl.ds(pl.multiple_of(index * size, size), size)


def kernel(
    groups,
    doms,
    rels,
    features,
    send_list,
    tile_values,
    tile_meta,
    rel_weight,
    self_weight,
    bn_gain,
    bn_shift,
    out,
    table,
    picked,
    message_out,
    message_in,
    adjacency,
    aggregated,
    weights,
    root,
    pre,
    group_stats,
    all_stats,
    result,
    own,
    own_sem,
    feature_sem,
    tile_sem,
    weight_sem,
    root_sem,
    message_send,
    message_recv,
    block_send,
    block_recv,
    group_send,
    group_recv,
    all_send,
    all_recv,
    out_sem,
):
    rows, width = features.shape
    kinds, _, hidden = rel_weight.shape
    block = tile_values.shape[-1]
    nblocks = rows // block
    slots = doms * rels
    sources = nblocks + doms
    chunks = width // F_CHUNK
    columns = hidden // COL_PARTS
    static = slots <= 16
    my_grp = lax.axis_index("grp")
    my_dom = lax.axis_index("dom")
    my_rel = lax.axis_index("rel")
    me = my_dom * rels + my_rel

    def peer(offset):
        target = lax.rem(me + offset, slots)
        return target // rels, lax.rem(target, rels)

    def group_peer(offset):
        dom, rel = peer(offset)
        return {"dom": dom, "rel": rel}

    def far_peer(offset):
        return {"grp": lax.rem(my_grp + offset, groups)}

    def tile_copy(offset):
        dom, rel = peer(offset)
        return pltpu.make_async_copy(
            tile_values.at[0, dom, rel],
            message_out.at[offset, pl.ds(0, block)],
            tile_sem.at[offset],
        )

    own_tile = pltpu.make_async_copy(
        tile_values.at[0, my_dom, my_rel], message_in.at[0, pl.ds(0, block)], tile_sem.at[0]
    )
    own_features = pltpu.make_async_copy(features, table.at[pl.ds(0, rows)], feature_sem)

    own_copy = pltpu.make_async_copy(features, own, own_sem)
    own_copy.start()
    own_features.start()
    repeat(slots - 1, lambda i: tile_copy(i + 1).start(), static)
    own_tile.start()

    barrier = pltpu.get_barrier_semaphore()

    def greet_group(i):
        pl.semaphore_signal(barrier, inc=1, device_id=group_peer(i + 1), device_id_type=MESH)

    def greet_far(i):
        pl.semaphore_signal(barrier, inc=1, device_id=far_peer(i + 1), device_id_type=MESH)

    repeat(slots - 1, greet_group, static)
    repeat(groups - 1, greet_far, static)

    root_copy = pltpu.make_async_copy(self_weight, root, root_sem)
    root_copy.start()

    def weight_copy(chunk, kind):
        return pltpu.make_async_copy(
            rel_weight.at[kind, pl.ds(chunk * F_CHUNK, F_CHUNK)],
            weights.at[chunk, pl.ds(kind * F_CHUNK, F_CHUNK)],
            weight_sem.at[chunk, kind],
        )

    for chunk in range(chunks):
        for kind in range(kinds):
            weight_copy(chunk, kind).start()

    def write_code(offset, ref):
        dom, rel = peer(offset)
        source = tile_meta[0, dom, rel, 2]
        around = dom - (source - nblocks)
        around = jnp.where(around < 0, around + doms, around)
        place = jnp.where(source < nblocks, source, nblocks + around)
        row = tile_meta[0, dom, rel, 0] * nblocks + tile_meta[0, dom, rel, 1]
        code = jnp.where(tile_meta[0, dom, rel, 3] != 0, row * sources + place, -1)
        splat = jnp.full((CODE_ROWS, block), code.astype(jnp.float32), jnp.float32)
        ref[offset, pl.ds(block, CODE_ROWS), :] = splat.astype(jnp.bfloat16)

    write_code(0, message_in)
    repeat(slots - 1, lambda i: write_code(i + 1, message_out), static)

    own_copy.wait()

    def pick(offset):
        chosen = send_list[0, lax.rem(my_dom + offset, doms), 0]
        chosen = jnp.full((block, width), chosen.astype(jnp.float32)).astype(jnp.bfloat16)
        total = own[pl.ds(0, block), :]
        for index in range(1, nblocks):
            here = own[pl.ds(index * block, block), :]
            total = jnp.where(chosen == jnp.bfloat16(index), here, total)
        return total

    for offset in range(1, doms):
        picked[offset - 1] = pick(offset)
    table[pl.ds(nblocks * block, block), :] = pick(0)

    pl.semaphore_wait(barrier, slots - 1 + groups - 1)

    def message_copy(offset):
        return pltpu.make_async_remote_copy(
            src_ref=message_out.at[offset],
            dst_ref=message_in.at[offset],
            send_sem=message_send.at[offset],
            recv_sem=message_recv.at[offset],
            device_id=group_peer(offset),
            device_id_type=MESH,
        )

    def send_message(i):
        tile_copy(i + 1).wait()
        message_copy(i + 1).start()

    repeat(slots - 1, send_message, static)

    def block_copy(offset, chunk):
        part = pl.ds(chunk * F_CHUNK, F_CHUNK)
        return pltpu.make_async_remote_copy(
            src_ref=picked.at[offset - 1, :, part],
            dst_ref=table.at[pl.ds((nblocks + offset) * block, block), part],
            send_sem=block_send.at[chunk, offset - 1],
            recv_sem=block_recv.at[chunk, offset - 1],
            device_id={"dom": lax.rem(my_dom + offset, doms)},
            device_id_type=MESH,
        )

    for chunk in range(chunks):
        for offset in range(1, doms):
            block_copy(offset, chunk).start()

    root_copy.wait()
    own_features.wait()
    pre[...] = jnp.dot(own[...], root[...], preferred_element_type=jnp.float32)

    own_tile.wait()
    repeat(slots - 1, lambda i: message_copy(i + 1).wait_recv(), static)

    zero = jnp.zeros((CODE_ROWS, block), jnp.bfloat16)

    def place_tile(row, source, strip):
        code = row * sources + source
        if static:
            total = zero
            wanted = jnp.bfloat16(code)
            for slot in range(slots):
                same = message_in[slot, pl.ds(block, CODE_ROWS), :] == wanted
                total = jnp.where(
                    same, message_in[slot, aligned(strip, CODE_ROWS), :], total
                )
        else:
            wanted = jnp.full((CODE_ROWS, block), code.astype(jnp.float32)).astype(jnp.bfloat16)

            def step(slot, total):
                same = message_in[slot, pl.ds(block, CODE_ROWS), :] == wanted
                return jnp.where(
                    same, message_in[slot, aligned(strip, CODE_ROWS), :], total
                )

            total = lax.fori_loop(0, slots, step, zero)
        first = pl.multiple_of(row * block + strip * CODE_ROWS, CODE_ROWS)
        adjacency[pl.ds(first, CODE_ROWS), aligned(source, block)] = total

    @pl.loop(0, block // CODE_ROWS)
    def _(strip):
        repeat(
            kinds * nblocks,
            lambda row: repeat(sources, lambda source: place_tile(row, source, strip), static),
            static,
        )

    def aggregate(chunk):
        for offset in range(1, doms):
            block_copy(offset, chunk).wait_recv()
        part = pl.ds(chunk * F_CHUNK, F_CHUNK)
        for kind in range(kinds):
            weight_copy(chunk, kind).wait()
        for kind in range(kinds):
            aggregated[:, pl.ds(kind * F_CHUNK, F_CHUNK)] = jnp.dot(
                adjacency[pl.ds(kind * rows, rows), :],
                table[:, part],
                preferred_element_type=jnp.float32,
            ).astype(jnp.bfloat16)

    for chunk in range(chunks - 1):
        aggregate(chunk)
        pre[...] += jnp.dot(
            aggregated[...], weights[chunk], preferred_element_type=jnp.float32
        )

    aggregate(chunks - 1)

    def group_copy(part, offset):
        return pltpu.make_async_remote_copy(
            src_ref=group_stats.at[part, 0],
            dst_ref=group_stats.at[part, offset],
            send_sem=group_send.at[part, offset],
            recv_sem=group_recv.at[part, offset],
            device_id=group_peer(offset),
            device_id_type=MESH,
        )

    def far_copy(part, offset):
        return pltpu.make_async_remote_copy(
            src_ref=all_stats.at[part, 0],
            dst_ref=all_stats.at[part, offset],
            send_sem=all_send.at[part, offset],
            recv_sem=all_recv.at[part, offset],
            device_id=far_peer(offset),
            device_id_type=MESH,
        )

    def combine(stats, part, count, each):
        entries = [stats[part, index] for index in range(count)]
        mean = sum(entry[0:1] for entry in entries) * (1.0 / count)
        spread = sum(entry[1:2] for entry in entries)
        apart = [entry[0:1] - mean for entry in entries]
        return mean, spread + sum(gap * gap for gap in apart) * each

    for part in range(COL_PARTS):
        span = pl.ds(part * columns, columns)
        value = pre[:, span] + jnp.dot(
            aggregated[...], weights[chunks - 1, :, span], preferred_element_type=jnp.float32
        )
        pre[:, span] = value
        mean = jnp.sum(value, axis=0, keepdims=True) * (1.0 / rows)
        centered = value - mean
        group_stats[part, 0, 0:1, :] = mean
        group_stats[part, 0, 1:2, :] = jnp.sum(centered * centered, axis=0, keepdims=True)
        repeat(slots - 1, lambda i: group_copy(part, i + 1).start(), static)

    for part in range(COL_PARTS):
        repeat(slots - 1, lambda i: group_copy(part, i + 1).wait_recv(), static)
        mean, spread = combine(group_stats, part, slots, float(rows))
        all_stats[part, 0, 0:1, :] = mean
        all_stats[part, 0, 1:2, :] = spread
        repeat(groups - 1, lambda i: far_copy(part, i + 1).start(), static)

    copies = []
    for part in range(COL_PARTS):
        span = pl.ds(part * columns, columns)
        repeat(groups - 1, lambda i: far_copy(part, i + 1).wait_recv(), static)
        mean, spread = combine(all_stats, part, groups, float(rows * slots))
        variance = spread * (1.0 / (rows * slots * groups))
        scale = bn_gain[:, span] / jnp.sqrt(variance + 1e-05)
        normed = (pre[:, span] - mean) * scale + bn_shift[:, span]
        below = jnp.exp(jnp.minimum(normed, 0.0)) - 1.0
        result[:, span] = jnp.where(normed > 0, normed, below).astype(jnp.bfloat16)
        copy = pltpu.make_async_copy(result.at[:, span], out.at[:, span], out_sem.at[part])
        copy.start()
        copies.append(copy)

    repeat(slots - 1, lambda i: message_copy(i + 1).wait_send(), static)
    for chunk in range(chunks):
        for offset in range(1, doms):
            block_copy(offset, chunk).wait_send()
    for part in range(COL_PARTS):
        repeat(slots - 1, lambda i: group_copy(part, i + 1).wait_send(), static)
        repeat(groups - 1, lambda i: far_copy(part, i + 1).wait_send(), static)
    for copy in copies:
        copy.wait()


def body(features, send_list, tile_values, tile_meta, rel_weight, self_weight, bn_gain, bn_shift):
    rows, width = features.shape
    kinds, _, hidden = rel_weight.shape
    block = tile_values.shape[-1]
    nblocks = rows // block
    groups = lax.axis_size("grp")
    doms = lax.axis_size("dom")
    rels = lax.axis_size("rel")
    slots = doms * rels
    sources = nblocks + doms
    chunks = width // F_CHUNK
    columns = hidden // COL_PARTS
    anywhere = pl.BlockSpec(memory_space=pl.ANY)
    scalars = pl.BlockSpec(memory_space=pltpu.SMEM)
    local = pl.BlockSpec(memory_space=pltpu.VMEM)
    dma = pltpu.SemaphoreType.DMA
    return pl.pallas_call(
        functools.partial(kernel, groups, doms, rels),
        out_shape=jax.ShapeDtypeStruct((rows, hidden), jnp.bfloat16),
        in_specs=[anywhere, scalars, anywhere, scalars, anywhere, anywhere, local, local],
        out_specs=anywhere,
        scratch_shapes=[
            pltpu.VMEM((sources * block, width), jnp.bfloat16),
            pltpu.VMEM((doms - 1, block, width), jnp.bfloat16),
            pltpu.VMEM((slots, block + CODE_ROWS, block), jnp.bfloat16),
            pltpu.VMEM((slots, block + CODE_ROWS, block), jnp.bfloat16),
            pltpu.VMEM((kinds * rows, sources * block), jnp.bfloat16),
            pltpu.VMEM((rows, kinds * F_CHUNK), jnp.bfloat16),
            pltpu.VMEM((chunks, kinds * F_CHUNK, hidden), jnp.bfloat16),
            pltpu.VMEM((width, hidden), jnp.bfloat16),
            pltpu.VMEM((rows, hidden), jnp.float32),
            pltpu.VMEM((COL_PARTS, slots, 2, columns), jnp.float32),
            pltpu.VMEM((COL_PARTS, groups, 2, columns), jnp.float32),
            pltpu.VMEM((rows, hidden), jnp.bfloat16),
            pltpu.VMEM((rows, width), jnp.bfloat16),
            dma(()),
            dma(()),
            dma((slots,)),
            dma((chunks, kinds)),
            dma(()),
            dma((slots,)),
            dma((slots,)),
            dma((chunks, doms - 1)),
            dma((chunks, doms - 1)),
            dma((COL_PARTS, slots)),
            dma((COL_PARTS, slots)),
            dma((COL_PARTS, groups)),
            dma((COL_PARTS, groups)),
            dma((COL_PARTS,)),
        ],
        compiler_params=pltpu.CompilerParams(
            collective_id=0, has_side_effects=True, vmem_limit_bytes=48 * 1024 * 1024
        ),
        cost_estimate=pl.CostEstimate(
            flops=2 * rows * (kinds + 1) * width * hidden,
            bytes_accessed=2 * (kinds + 1) * width * hidden,
            transcendentals=rows * hidden,
        ),
    )(
        features,
        send_list,
        tile_values,
        tile_meta,
        rel_weight,
        self_weight,
        bn_gain.reshape(1, hidden),
        bn_shift.reshape(1, hidden),
    )


def solution(mesh):
    return jax.shard_map(
        body,
        mesh=mesh,
        in_specs=(
            P(("grp", "dom", "rel"), None),
            P(("grp", "dom", "rel"), None, None),
            P(("grp", "dom", "rel"), None, None, None, None),
            P(("grp", "dom", "rel"), None, None, None),
            P(),
            P(),
            P(),
            P(),
        ),
        out_specs=P(("grp", "dom", "rel"), None),
        check_vma=False,
    )
```

time: 134 us -> 32.7 us (0.24)
  blocking collectives: 79.7 us -> 0 us
  Pallas kernels: 0 us -> 25.5 us
  matrix products: 17.7 us -> 0 us
  waiting for transfers between devices: 12.4 us -> 0 us
  starting transfers between devices: 12.2 us -> 0 us
  other arithmetic: 2.23 us -> 0 us
  local copies, waits for them, and re-layouts: 8.5 us -> 6.95 us
    psum x2 -> x0, blocking collectives: 79.7 us -> none  [the longest x1 40.2 us: body(): lax.psum(jnp.sum(centered * centered, axis=0), ('grp', 'dom', 'rel'))]
    pallas_call x0 -> x1, Pallas kernels: none -> 25.5 us  [body(): pl.pallas_call(functools.partial(kernel, groups, doms, rels), out_shape=j...]
    dot_general x8 -> x0, matrix products: 17.7 us -> none  [the longest x1 7.04 us: accumulate(): jnp.einsum('kc,kif->cif', select, message, precision=lax.Precision.HIGHEST)]
    all_to_all x3 -> x0, waiting for transfers between devices: 12.4 us -> none  [the longest x1 7.39 us: body(): lax.all_to_all(outgoing, 'dom', split_axis=0, concat_axis=0, tiled=True)]
    all_to_all x3 -> x0, starting transfers between devices: 12.2 us -> none  [the longest x1 5.3 us: body(): lax.all_to_all(tile_meta.reshape(slots, 4), ('dom', 'rel'), split_axis=0,...]
    unnamed x14, local copies, waits for them, and re-layouts: 0.04 us -> 6.95 us
    dot_general x1 -> x0, local copies, waits for them, and re-layouts: 3.68 us -> none  [accumulate(): jnp.einsum('kij,kjf->kif', tile_group, sources, preferred_element_type=jn...]
    gather x2 -> x0, local copies, waits for them, and re-layouts: 3.12 us -> none  [the longest x1 1.8 us: accumulate(): sources = table[meta_group[:, 2]]]
  transfers between devices with their start and end apart: 3 -> 0, of which waited for: 2 -> 0; matrix products, arithmetic and copies ran while one was open for 5% -> 0% of each run, Pallas kernels for 0% -> 0%
where the time goes in v1:
time: 32.7 us; the launch traced here: 32.4 us
  Pallas kernels  25.5 us (78%)
  local copies, waits for them, and re-layouts  6.95 us (21%)
    pallas_call x1, Pallas kernels, body(): pl.pallas_call(functools.partial(kernel, groups, doms, rels), out_shape=j...  25.5 us
    unnamed x14, local copies, waits for them, and re-layouts  6.95 us

profile of v1, /device:TPU:0, one launch (start us, length us, event | category | flops | bytes accessed | tf_op | source)
XLA Modules:
  0.0 32.4 jit_solution(5303774624682494549)
XLA Ops:
  0.0 0.7 %copy.9.send_list = s32[1,2,1]{2,1,0:T(2,128)S(1)} copy(s32[1,2,1]{1,2,0:T(1,128)} %param.9) | data formatting | bytes 16 | tf_op args[1]
  0.7 0.0 copy-start
  0.7 1.4 %copy-done = bf16[768,1024]{1,0:T(8,128)(2,1)S(1)} copy-done((bf16[768,1024]{1,0:T(8,128)(2,1)S(1)}, bf16[768,1024]{1,0:T(8,128)(2,1)}, u32[]{:S(2)}) %copy-start) | copy-done | bytes 1572888
  2.1 0.0 copy-start.1
  2.2 1.0 %copy-done.1 = bf16[256,768]{1,0:T(8,128)(2,1)S(1)} copy-done((bf16[256,768]{1,0:T(8,128)(2,1)S(1)}, bf16[256,768]{1,0:T(8,128)(2,1)}, u32[]{:S(2)}) %copy-start.1) | copy-done | bytes 393240
  3.1 0.0 copy-start.2
  3.1 0.9 %copy-done.2 = bf16[1,2,4,128,128]{4,3,2,1,0:T(8,128)(2,1)S(1)} copy-done((bf16[1,2,4,128,128]{4,3,2,1,0:T(8,128)(2,1)S(1)}, bf16[1,2,4,128,128]{4,3,2,1,0:T(8,128)(2,1)}, u32[]{:S(2)}) %copy-start.2) | copy-done | bytes 262168
  4.1 0.0 copy-start.3
  4.1 0.7 %copy-done.3 = s32[1,2,4,4]{3,2,1,0:T(4,128)S(1)} copy-done((s32[1,2,4,4]{3,2,1,0:T(4,128)S(1)}, s32[1,2,4,4]{3,2,1,0:T(4,128)}, u32[]{:S(2)}) %copy-start.3) | copy-done | bytes 152
  4.8 0.0 copy-start.4
  4.8 0.7 %copy-done.4 = f32[1024]{0:T(1024)S(1)} copy-done((f32[1024]{0:T(1024)S(1)}, f32[1024]{0:T(1024)}, u32[]{:S(2)}) %copy-start.4) | copy-done | bytes 4120
  5.5 0.0 copy-start.5
  5.5 0.7 %copy-done.5 = f32[1024]{0:T(1024)S(1)} copy-done((f32[1024]{0:T(1024)S(1)}, f32[1024]{0:T(1024)}, u32[]{:S(2)}) %copy-start.5) | copy-done | bytes 4120
  6.2 25.5 %shard_map.82 = bf16[256,1024]{1,0:T(8,128)(2,1)S(1)} custom-call(bf16[256,768]{1,0:T(8,128)(2,1)S(1)} %copy-done.1, s32[1,2,1]{2,1,0:T(2,128)S(1)} %copy.9.send_list, bf16[1,2,4,128,128]{4,3,2,1,0:T(8,128)(2,1)S(1)} %copy-done.2, s32[1,2,4,4]{3,2,1,0:T(4,128)S(1)} %copy-done.3, bf16[5,768,1024]{2,1,0:T(8,128)(2,1)} %rel_weight.1, ...), custom_call_target="tpu_custom_call" | custom-call | flops 2415919104 | bytes 9437184 | tf_op jit(solution)/shard_map/pallas_call | solution.py:351
  31.6 0.8 %copy.11 = bf16[256,1024]{1,0:T(8,128)(2,1)} copy(bf16[256,1024]{1,0:T(8,128)(2,1)S(1)} %shard_map.82) | data formatting | bytes 1048576
Async XLA Ops:
  0.7 1.4 %copy-start = (bf16[768,1024]{1,0:T(8,128)(2,1)S(1)}, bf16[768,1024]{1,0:T(8,128)(2,1)}, u32[]{:S(2)}) copy-start(bf16[768,1024]{1,0:T(8,128)(2,1)} %self_weight.1) | copy-start | bytes 4718596
  2.1 1.0 %copy-start.1 = (bf16[256,768]{1,0:T(8,128)(2,1)S(1)}, bf16[256,768]{1,0:T(8,128)(2,1)}, u32[]{:S(2)}) copy-start(bf16[256,768]{1,0:T(8,128)(2,1)} %features.1) | copy-start | bytes 1179652
  3.1 0.9 %copy-start.2 = (bf16[1,2,4,128,128]{4,3,2,1,0:T(8,128)(2,1)S(1)}, bf16[1,2,4,128,128]{4,3,2,1,0:T(8,128)(2,1)}, u32[]{:S(2)}) copy-start(bf16[1,2,4,128,128]{4,3,2,1,0:T(8,128)(2,1)} %tile_values.1) | copy-start | bytes 786436
  4.1 0.7 %copy-start.3 = (s32[1,2,4,4]{3,2,1,0:T(4,128)S(1)}, s32[1,2,4,4]{3,2,1,0:T(4,128)}, u32[]{:S(2)}) copy-start(s32[1,2,4,4]{3,2,1,0:T(4,128)} %tile_meta.1) | copy-start | bytes 388
  4.8 0.7 %copy-start.4 = (f32[1024]{0:T(1024)S(1)}, f32[1024]{0:T(1024)}, u32[]{:S(2)}) copy-start(f32[1024]{0:T(1024)} %param.14) | copy-start | bytes 12292
  5.5 0.7 %copy-start.5 = (f32[1024]{0:T(1024)S(1)}, f32[1024]{0:T(1024)}, u32[]{:S(2)}) copy-start(f32[1024]{0:T(1024)} %param.15) | copy-start | bytes 12292

commit v2 on v1

--- a/solution.py
+++ b/solution.py
@@ -10,7 +10,7 @@
 MESH = pl.DeviceIdType.MESH
 CODE_ROWS = 16
 F_CHUNK = 256
-COL_PARTS = 2
+COL_PARTS = 1
 
 
 def repeat(count, body, static):
@@ -33,14 +33,18 @@
     doms,
     rels,
     features,
-    send_list,
+    send_list_hbm,
     tile_values,
-    tile_meta,
+    tile_meta_hbm,
     rel_weight,
     self_weight,
+    bn_gain_hbm,
+    bn_shift_hbm,
+    result,
+    send_list,
+    tile_meta,
     bn_gain,
     bn_shift,
-    out,
     table,
     picked,
     message_out,
@@ -52,8 +56,8 @@
     pre,
     group_stats,
     all_stats,
-    result,
     own,
+    small_sem,
     own_sem,
     feature_sem,
     tile_sem,
@@ -67,7 +71,6 @@
     group_recv,
     all_send,
     all_recv,
-    out_sem,
 ):
     rows, width = features.shape
     kinds, _, hidden = rel_weight.shape
@@ -107,6 +110,19 @@
     )
     own_features = pltpu.make_async_copy(features, table.at[pl.ds(0, rows)], feature_sem)
 
+    small_copies = [
+        pltpu.make_async_copy(source, target, small_sem.at[index])
+        for index, (source, target) in enumerate(
+            (
+                (send_list_hbm, send_list),
+                (tile_meta_hbm, tile_meta),
+                (bn_gain_hbm, bn_gain),
+                (bn_shift_hbm, bn_shift),
+            )
+        )
+    ]
+    for copy in small_copies:
+        copy.start()
     own_copy = pltpu.make_async_copy(features, own, own_sem)
     own_copy.start()
     own_features.start()
@@ -149,13 +165,15 @@
         splat = jnp.full((CODE_ROWS, block), code.astype(jnp.float32), jnp.float32)
         ref[offset, pl.ds(block, CODE_ROWS), :] = splat.astype(jnp.bfloat16)
 
+    for copy in small_copies:
+        copy.wait()
     write_code(0, message_in)
     repeat(slots - 1, lambda i: write_code(i + 1, message_out), static)
 
     own_copy.wait()
 
     def pick(offset):
-        chosen = send_list[0, lax.rem(my_dom + offset, doms), 0]
+        chosen = send_list[0, lax.rem(my_dom + offset, doms)]
         chosen = jnp.full((block, width), chosen.astype(jnp.float32)).astype(jnp.bfloat16)
         total = own[pl.ds(0, block), :]
         for index in range(1, nblocks):
@@ -307,7 +325,6 @@
         all_stats[part, 0, 1:2, :] = spread
         repeat(groups - 1, lambda i: far_copy(part, i + 1).start(), static)
 
-    copies = []
     for part in range(COL_PARTS):
         span = pl.ds(part * columns, columns)
         repeat(groups - 1, lambda i: far_copy(part, i + 1).wait_recv(), static)
@@ -317,9 +334,6 @@
         normed = (pre[:, span] - mean) * scale + bn_shift[:, span]
         below = jnp.exp(jnp.minimum(normed, 0.0)) - 1.0
         result[:, span] = jnp.where(normed > 0, normed, below).astype(jnp.bfloat16)
-        copy = pltpu.make_async_copy(result.at[:, span], out.at[:, span], out_sem.at[part])
-        copy.start()
-        copies.append(copy)
 
     repeat(slots - 1, lambda i: message_copy(i + 1).wait_send(), static)
     for chunk in range(chunks):
@@ -328,8 +342,6 @@
     for part in range(COL_PARTS):
         repeat(slots - 1, lambda i: group_copy(part, i + 1).wait_send(), static)
         repeat(groups - 1, lambda i: far_copy(part, i + 1).wait_send(), static)
-    for copy in copies:
-        copy.wait()
 
 
 def body(features, send_list, tile_values, tile_meta, rel_weight, self_weight, bn_gain, bn_shift):
@@ -344,16 +356,18 @@
     sources = nblocks + doms
     chunks = width // F_CHUNK
     columns = hidden // COL_PARTS
-    anywhere = pl.BlockSpec(memory_space=pl.ANY)
-    scalars = pl.BlockSpec(memory_space=pltpu.SMEM)
-    local = pl.BlockSpec(memory_space=pltpu.VMEM)
+    anywhere = pl.BlockSpec(memory_space=pltpu.HBM)
     dma = pltpu.SemaphoreType.DMA
     return pl.pallas_call(
         functools.partial(kernel, groups, doms, rels),
         out_shape=jax.ShapeDtypeStruct((rows, hidden), jnp.bfloat16),
-        in_specs=[anywhere, scalars, anywhere, scalars, anywhere, anywhere, local, local],
-        out_specs=anywhere,
+        in_specs=[anywhere] * 8,
+        out_specs=pl.BlockSpec(memory_space=pltpu.VMEM),
         scratch_shapes=[
+            pltpu.SMEM((1, doms), jnp.int32),
+            pltpu.SMEM(tile_meta.shape, jnp.int32),
+            pltpu.VMEM((1, hidden), jnp.float32),
+            pltpu.VMEM((1, hidden), jnp.float32),
             pltpu.VMEM((sources * block, width), jnp.bfloat16),
             pltpu.VMEM((doms - 1, block, width), jnp.bfloat16),
             pltpu.VMEM((slots, block + CODE_ROWS, block), jnp.bfloat16),
@@ -365,8 +379,8 @@
             pltpu.VMEM((rows, hidden), jnp.float32),
             pltpu.VMEM((COL_PARTS, slots, 2, columns), jnp.float32),
             pltpu.VMEM((COL_PARTS, groups, 2, columns), jnp.float32),
-            pltpu.VMEM((rows, hidden), jnp.bfloat16),
             pltpu.VMEM((rows, width), jnp.bfloat16),
+            dma((4,)),
             dma(()),
             dma(()),
             dma((slots,)),
@@ -380,10 +394,9 @@
             dma((COL_PARTS, slots)),
             dma((COL_PARTS, groups)),
             dma((COL_PARTS, groups)),
-            dma((COL_PARTS,)),
         ],
         compiler_params=pltpu.CompilerParams(
-            collective_id=0, has_side_effects=True, vmem_limit_bytes=48 * 1024 * 1024
+            collective_id=0, has_side_effects=True, vmem_limit_bytes=62 * 1024 * 1024
         ),
         cost_estimate=pl.CostEstimate(
             flops=2 * rows * (kinds + 1) * width * hidden,
@@ -392,7 +405,7 @@
         ),
     )(
         features,
-        send_list,
+        send_list.reshape(1, doms),
         tile_values,
         tile_meta,
         rel_weight,

time: 32.7 us -> 26.6 us (0.81)
  local copies, waits for them, and re-layouts: 6.95 us -> 1.87 us
  Pallas kernels: 25.5 us -> 24.6 us
    unnamed x14 -> x1, local copies, waits for them, and re-layouts: 6.95 us -> 1.87 us
    pallas_call x1, Pallas kernels: 25.5 us -> 24.6 us  [body(): pl.pallas_call(functools.partial(kernel, groups, doms, rels), out_shape=j...]
where the time goes in v2:
time: 26.6 us; the launch traced here: 26.5 us
  Pallas kernels  24.6 us (92%)
  local copies, waits for them, and re-layouts  1.87 us (7%)
    pallas_call x1, Pallas kernels, body(): pl.pallas_call(functools.partial(kernel, groups, doms, rels), out_shape=j...  24.6 us
    unnamed x1, local copies, waits for them, and re-layouts  1.87 us

profile of v2, /device:TPU:0, one launch (start us, length us, event | category | flops | bytes accessed | tf_op | source)
XLA Modules:
  0.0 26.5 jit_solution(713901544734255026)
XLA Ops:
  0.0 24.6 %shard_map.82 = bf16[256,1024]{1,0:T(8,128)(2,1)} custom-call(bf16[256,768]{1,0:T(8,128)(2,1)} %features.1, s32[1,2]{1,0:T(1,128)} %bitcast.5, bf16[1,2,4,128,128]{4,3,2,1,0:T(8,128)(2,1)} %tile_values.1, s32[1,2,4,4]{3,2,1,0:T(4,128)} %tile_meta_hbm.1, bf16[5,768,1024]{2,1,0:T(8,128)(2,1)} %rel_weight.1, bf16[768,1024]{1,0:T(8,128)(2,1)} %self_weight.1, ...), custom_call_target="tpu_custom_call" | custom-call | flops 2415919104 | bytes 9437184 | tf_op jit(solution)/shard_map/pallas_call | solution.py:361
  24.6 1.9 %copy.10 = bf16[256,1024]{1,0:T(8,128)(2,1)} copy(bf16[256,1024]{1,0:T(8,128)(2,1)} %shard_map.82) | data formatting | bytes 1048576

commit v3 on v2

--- a/solution.py
+++ b/solution.py
@@ -11,6 +11,7 @@
 CODE_ROWS = 16
 F_CHUNK = 256
 COL_PARTS = 1
+ROW_PARTS = 4
 
 
 def repeat(count, body, static):
@@ -40,7 +41,7 @@
     self_weight,
     bn_gain_hbm,
     bn_shift_hbm,
-    result,
+    out,
     send_list,
     tile_meta,
     bn_gain,
@@ -57,6 +58,8 @@
     group_stats,
     all_stats,
     own,
+    result,
+    out_sem,
     small_sem,
     own_sem,
     feature_sem,
@@ -325,15 +328,23 @@
         all_stats[part, 0, 1:2, :] = spread
         repeat(groups - 1, lambda i: far_copy(part, i + 1).start(), static)
 
+    copies = []
     for part in range(COL_PARTS):
         span = pl.ds(part * columns, columns)
         repeat(groups - 1, lambda i: far_copy(part, i + 1).wait_recv(), static)
         mean, spread = combine(all_stats, part, groups, float(rows * slots))
         variance = spread * (1.0 / (rows * slots * groups))
         scale = bn_gain[:, span] / jnp.sqrt(variance + 1e-05)
-        normed = (pre[:, span] - mean) * scale + bn_shift[:, span]
-        below = jnp.exp(jnp.minimum(normed, 0.0)) - 1.0
-        result[:, span] = jnp.where(normed > 0, normed, below).astype(jnp.bfloat16)
+        for quarter in range(ROW_PARTS):
+            strip = pl.ds(quarter * (rows // ROW_PARTS), rows // ROW_PARTS)
+            normed = (pre[strip, span] - mean) * scale + bn_shift[:, span]
+            below = jnp.exp(jnp.minimum(normed, 0.0)) - 1.0
+            result[strip, span] = jnp.where(normed > 0, normed, below).astype(jnp.bfloat16)
+            copy = pltpu.make_async_copy(
+                result.at[strip, span], out.at[strip, span], out_sem.at[part, quarter]
+            )
+            copy.start()
+            copies.append(copy)
 
     repeat(slots - 1, lambda i: message_copy(i + 1).wait_send(), static)
     for chunk in range(chunks):
@@ -342,6 +353,8 @@
     for part in range(COL_PARTS):
         repeat(slots - 1, lambda i: group_copy(part, i + 1).wait_send(), static)
         repeat(groups - 1, lambda i: far_copy(part, i + 1).wait_send(), static)
+    for copy in copies:
+        copy.wait()
 
 
 def body(features, send_list, tile_values, tile_meta, rel_weight, self_weight, bn_gain, bn_shift):
@@ -362,7 +375,7 @@
         functools.partial(kernel, groups, doms, rels),
         out_shape=jax.ShapeDtypeStruct((rows, hidden), jnp.bfloat16),
         in_specs=[anywhere] * 8,
-        out_specs=pl.BlockSpec(memory_space=pltpu.VMEM),
+        out_specs=anywhere,
         scratch_shapes=[
             pltpu.SMEM((1, doms), jnp.int32),
             pltpu.SMEM(tile_meta.shape, jnp.int32),
@@ -380,6 +393,8 @@
             pltpu.VMEM((COL_PARTS, slots, 2, columns), jnp.float32),
             pltpu.VMEM((COL_PARTS, groups, 2, columns), jnp.float32),
             pltpu.VMEM((rows, width), jnp.bfloat16),
+            pltpu.VMEM((rows, hidden), jnp.bfloat16),
+            dma((COL_PARTS, ROW_PARTS)),
             dma((4,)),
             dma(()),
             dma(()),

time: 26.6 us -> 26.5 us (level)
  no operation moved by 1% of the time
where the time goes in v3:
time: 26.5 us; the launch traced here: 26.4 us
  Pallas kernels  24.5 us (92%)
  local copies, waits for them, and re-layouts  1.87 us (7%)
    pallas_call x1, Pallas kernels, body(): pl.pallas_call(functools.partial(kernel, groups, doms, rels), out_shape=j...  24.5 us
    unnamed x1, local copies, waits for them, and re-layouts  1.87 us

profile of v3, /device:TPU:0, one launch (start us, length us, event | category | flops | bytes accessed | tf_op | source)
XLA Modules:
  0.0 26.4 jit_solution(8474420638976032442)
XLA Ops:
  0.0 24.5 %shard_map.82 = bf16[256,1024]{1,0:T(8,128)(2,1)} custom-call(bf16[256,768]{1,0:T(8,128)(2,1)} %features.1, s32[1,2]{1,0:T(1,128)} %bitcast.5, bf16[1,2,4,128,128]{4,3,2,1,0:T(8,128)(2,1)} %tile_values.1, s32[1,2,4,4]{3,2,1,0:T(4,128)} %tile_meta_hbm.1, bf16[5,768,1024]{2,1,0:T(8,128)(2,1)} %rel_weight.1, bf16[768,1024]{1,0:T(8,128)(2,1)} %self_weight.1, ...), custom_call_target="tpu_custom_call" | custom-call | flops 2415919104 | bytes 9437184 | tf_op jit(solution)/shard_map/pallas_call | solution.py:374
  24.5 1.9 %copy.10 = bf16[256,1024]{1,0:T(8,128)(2,1)} copy(bf16[256,1024]{1,0:T(8,128)(2,1)} %shard_map.82) | data formatting | bytes 1048576
